TPU v7x, 128 devices: a whole 4x4x4 slice. The times are simulated.
128 devices in a mesh: lat: 32 (over y, x, core), swath: 4 (over z).
Axes of the slice: x: 4, y: 4, z: 4, core: 2. Of those that a mesh axis runs over, the one named last changes fastest.
Arguments:
- saved_state: float32 [6, 16, 512, 1024], P(None, None, 'lat', 'swath'), may hold values from 0.35 to 0.45
- background_increment: float32 [16, 512, 1024], P(None, 'lat', 'swath'), may hold values from -2.5 to 2.5
- obs_residual: float32 [128, 128, 6, 128], P(('lat', 'swath')), may hold values from -6 to 6
- obs_weight: float32 [128, 128, 6, 128], P(('lat', 'swath')), may hold values from 0.3 to 3
- obs_kernel: float32 [128, 128, 6, 4, 128], P(('lat', 'swath')), may hold values from 0.1 to 1
- obs_cell: int32 [128, 128, 6, 128], P(('lat', 'swath')), may hold values from 0 to 1023
- obs_count: int32 [128, 128, 6], P(('lat', 'swath')), may hold values from 0 to 128, as said below
Outputs:
- gradient: float32 [16, 512, 1024], P(None, 'lat', 'swath')
Inputs may be any that keep to these rules, and one draw needn't show every extreme that they name: `obs_count`: slots at or beyond the count are padding. In every step one tile receives 128 footprints from every owner.
All inputs are finite; a program needn't handle non-finite values.
Results may differ from a plain program's by a relative error of at most 0.00011.
Values sent between devices are 32-bit elements; how exact they have to be, the bound alone decides.
A program may use at most 128 MiB of HBM per device.

v0:
```python
import functools

import jax
import jax.numpy as jnp
from jax import lax
from jax.experimental import pallas as pl
from jax.experimental.pallas import tpu as pltpu
from jax.sharding import PartitionSpec as P

MESH = pl.DeviceIdType.MESH
F32 = jnp.float32
BF16 = jnp.bfloat16

SAT = 0.45
STEPS = 6
NZ = 16
ROWS = 16
LANES = 128
HALVES = 2
FOOT = 4

NY4 = 4
NI = 8
NZ4 = 4
NA = NY4 * NZ4


def iota(shape, dim):
    return lax.broadcasted_iota(jnp.int32, shape, dim)


def kernel(
    sv, bg, res, wgt, cell, ker, cnt, out,
    S, R, W, C, KV, CT, sendA, recvA, sendB, recvB, SHs, SHr, HS, HR,
    CF, KK, BG, V, E, PRE,
    in_sem, st_sem, a_send, a_recv, b_send, b_recv, sh_send, sh_recv, h_send, h_recv,
):
    lat = lax.axis_index("lat")
    z = lax.axis_index("swath")
    y = lat // NI
    me_i = lat % NI
    nlat = NY4 * NI

    loads = [
        pltpu.make_async_copy(res, R, in_sem.at[0]),
        pltpu.make_async_copy(wgt, W, in_sem.at[1]),
        pltpu.make_async_copy(cell, C, in_sem.at[2]),
        pltpu.make_async_copy(ker, KV, in_sem.at[3]),
    ]
    states = []
    for h in range(HALVES):
        cols = pl.ds(h * LANES, LANES)
        states.append(
            pltpu.make_async_copy(
                sv.at[:, :, :, cols], S.at[pl.ds(0, STEPS), h], st_sem.at[h]
            )
        )
        states.append(pltpu.make_async_copy(bg.at[:, :, cols], S.at[STEPS, h], st_sem.at[2 + h]))
    for c in states:
        c.start()
    for c in loads:
        c.start()

    barrier = pltpu.get_barrier_semaphore()
    for r in range(1, NA):
        ty = (y + r // NZ4) % NY4
        tz = (z + r % NZ4) % NZ4
        pl.semaphore_signal(barrier, inc=1, device_id=(ty * NI + me_i, tz), device_id_type=MESH)
    for k in range(1, NI):
        pl.semaphore_signal(
            barrier, inc=1, device_id=(y * NI + (me_i + k) % NI, z), device_id_type=MESH
        )
    up = (lat + nlat - 1) % nlat
    down = (lat + 1) % nlat
    left = (z + NZ4 - 1) % NZ4
    right = (z + 1) % NZ4
    pl.semaphore_signal(barrier, inc=1, device_id=(up, z), device_id_type=MESH)
    pl.semaphore_signal(barrier, inc=1, device_id=(down, z), device_id_type=MESH)

    lane8 = iota((8, LANES), 1)
    lane = iota((ROWS, LANES), 1)
    row = iota((ROWS, LANES), 0)

    counts = jnp.concatenate([cnt[...].astype(F32), jnp.zeros((LANES - STEPS, LANES), F32)], 0)
    CT[...] = jnp.transpose(counts, (1, 0))

    def build(q, carry):
        rr = iota((LANES, 512), 0)
        cc = iota((LANES, 512), 1)
        hit = ((rr >> 6) == (cc >> 8)) & (((rr & 63) * FOOT + q) == (cc & 255))
        E[pl.ds(pl.multiple_of(q * LANES, LANES), LANES), :] = jnp.where(hit, 1.0, 0.0).astype(BF16)
        return carry

    lax.fori_loop(0, FOOT, build, 0)

    for c in states:
        c.wait()

    S2 = S.reshape((STEPS + 1) * HALVES * NZ * ROWS, LANES)

    def state_edges(t, carry):
        for h in range(HALVES):
            base = (t * HALVES + h) * NZ * ROWS
            SHs[t, h] = S2[pl.ds(base + ROWS - 1, NZ, stride=ROWS), :]
            SHs[t, 2 + h] = S2[pl.ds(base, NZ, stride=ROWS), :]
        p4 = jnp.zeros((ROWS, LANES), F32)
        p5 = jnp.zeros((ROWS, LANES), F32)
        for l in range(NZ):
            p4 = jnp.where(lane == l, S[t, 1, l][:, LANES - 1:], p4)
            p5 = jnp.where(lane == l, S[t, 0, l][:, :1], p5)
        SHs[t, 4] = p4
        SHs[t, 5] = p5
        return carry

    lax.fori_loop(0, STEPS + 1, state_edges, 0)

    pl.semaphore_wait(barrier, NA - 1 + NI - 1 + 2)

    routes = ((0, 2, (down, z)), (2, 2, (up, z)), (4, 1, (lat, right)), (5, 1, (lat, left)))

    def state_copies():
        return [
            pltpu.make_async_remote_copy(
                src_ref=SHs.at[:, pl.ds(first, many)],
                dst_ref=SHr.at[:, pl.ds(first, many)],
                send_sem=sh_send.at[n],
                recv_sem=sh_recv.at[n],
                device_id=to,
                device_id_type=MESH,
            )
            for n, (first, many, to) in enumerate(routes)
        ]

    for c in state_copies():
        c.start()

    for c in loads:
        c.wait()

    def weigh(t, yp, zp):
        d0 = yp * 32 + zp
        rows = pl.ds(t * LANES + d0, NI, stride=4)
        held = jnp.sum(jnp.where(lane8 == t, CT[pl.ds(d0, NI, stride=4), :], 0.0), 1, keepdims=True)
        scaled = jnp.where(lane8.astype(F32) < held, R[rows, :] * W[rows, :], 0.0)
        parts = [
            scaled * KV[pl.ds(d0 * STEPS * FOOT + t * FOOT + j, NI, stride=4 * STEPS * FOOT), :]
            for j in range(FOOT)
        ]
        return parts + [C[rows, :].astype(F32)]

    def stage_a_step(s, carry):
        t = STEPS - 1 - s

        def one(r, carry):
            ty = (y + r // NZ4) % NY4
            tz = (z + r % NZ4) % NZ4
            for q, part in enumerate(weigh(t, ty, tz)):
                sendA[t, r - 1, q] = part
            pltpu.make_async_remote_copy(
                src_ref=sendA.at[t, r - 1],
                dst_ref=recvA.at[t, r - 1],
                send_sem=a_send,
                recv_sem=a_recv.at[t],
                device_id=(ty * NI + me_i, tz),
                device_id_type=MESH,
            ).start()
            return carry

        lax.fori_loop(1, NA, one, 0)
        for q, part in enumerate(weigh(t, y, z)):
            recvA[t, NA - 1, q] = part
        return carry

    lax.fori_loop(0, STEPS, stage_a_step, 0)

    for c in state_copies():
        c.wait_recv()

    has_up = (lat > 0).astype(F32)
    has_down = (lat < nlat - 1).astype(F32)
    has_left = (z > 0).astype(F32)
    has_right = (z < NZ4 - 1).astype(F32)

    def cube(x):
        rel = x * (1.0 / SAT)
        return rel * rel * rel

    def around(halves, tops, bottoms, lefts, rights, h):
        x = halves[h]
        above = jnp.where(row == 0, tops[h], pltpu.roll(x, 1, 0))
        below = jnp.where(row == ROWS - 1, bottoms[h], pltpu.roll(x, ROWS - 1, 0))
        before = lefts if h == 0 else pltpu.roll(halves[0], 1, 1)
        before = jnp.where(lane == 0, before, pltpu.roll(x, 1, 1))
        after = rights if h == 1 else pltpu.roll(halves[1], LANES - 1, 1)
        after = jnp.where(lane == LANES - 1, after, pltpu.roll(x, LANES - 1, 1))
        return above, below, before, after

    def coefficients(s, carry):
        t = STEPS - 1 - s
        for l in range(NZ):
            for h in range(HALVES):
                KK[h, l] = cube(S[t, h, l])
        tops = [cube(SHr[t, h]) * has_up for h in range(HALVES)]
        bottoms = [cube(SHr[t, 2 + h]) * has_down for h in range(HALVES)]
        lefts = cube(SHr[t, 4]) * has_left
        rights = cube(SHr[t, 5]) * has_right
        for l in range(NZ):
            halves = [KK[0, l], KK[1, l]]
            for h in range(HALVES):
                k = halves[h]
                near = around(
                    halves,
                    [x[l:l + 1] for x in tops],
                    [x[l:l + 1] for x in bottoms],
                    lefts[:, l:l + 1],
                    rights[:, l:l + 1],
                    h,
                )
                cs = [0.05 * (k + x) for x in near]
                total = (cs[0] + cs[1]) + (cs[2] + cs[3])
                cs[0] = jnp.where(row == 0, cs[0] * has_up, cs[0])
                cs[1] = jnp.where(row == ROWS - 1, cs[1] * has_down, cs[1])
                if h == 0:
                    cs[2] = jnp.where(lane == 0, cs[2] * has_left, cs[2])
                else:
                    cs[3] = jnp.where(lane == LANES - 1, cs[3] * has_right, cs[3])
                rel = S[t, h, l] * (1.0 / SAT)
                drain = (0.03 * 3.0) * rel * rel
                total = total + drain
                for n in range(4):
                    CF[t, 1 + n, h, l] = cs[n]
                if l > 0:
                    over = 0.125 * (k + KK[h, l - 1])
                    CF[t, 5, h, l] = over
                    total = total + over
                if l < NZ - 1:
                    under = 0.125 * (k + KK[h, l + 1])
                    CF[t, 6, h, l] = under + drain
                    total = total + under
                CF[t, 0, h, l] = 1.0 - total
        return carry

    lax.fori_loop(0, STEPS, coefficients, 0)

    tops = [SHr[STEPS, h] * has_up for h in range(HALVES)]
    bottoms = [SHr[STEPS, 2 + h] * has_down for h in range(HALVES)]
    lefts = SHr[STEPS, 4] * has_left
    rights = SHr[STEPS, 5] * has_right
    for l in range(NZ):
        halves = [S[STEPS, 0, l], S[STEPS, 1, l]]
        for h in range(HALVES):
            near = around(
                halves,
                [x[l:l + 1] for x in tops],
                [x[l:l + 1] for x in bottoms],
                lefts[:, l:l + 1],
                rights[:, l:l + 1],
                h,
            )
            BG[h, l] = 0.9 * halves[h] - 0.1 * ((near[0] + near[1]) + (near[2] + near[3]))

    V[...] = jnp.zeros_like(V)

    n_iota = iota((LANES, LANES), 0).astype(F32).astype(BF16)
    a_iota = iota((8, LANES), 0).astype(F32)

    def gather(t):
        pltpu.make_async_copy(
            recvA.at[t, pl.ds(0, NA - 1)], recvA.at[t, pl.ds(0, NA - 1)], a_recv.at[t]
        ).wait()

        def split(o, carry):
            anchor = recvA[t, o, FOOT]
            r = jnp.floor(anchor * (1.0 / 64.0))
            b = jnp.floor(anchor * (1.0 / 512.0))
            PRE[o, 8] = (anchor - 64.0 * r) + 64.0 * b
            PRE[o, 9] = r - 8.0 * b
            for j in range(FOOT):
                v = recvA[t, o, j]
                hi = v.astype(BF16).astype(F32)
                PRE[o, 2 * j] = hi
                PRE[o, 2 * j + 1] = v - hi
            return carry

        lax.fori_loop(0, NA, split, 0)

        def tile(k, carry):
            i = (me_i + k) % NI
            acc = jnp.zeros((FOOT * 16, LANES), F32)
            for o in range(0, NA, 2):
                lhs, rhs = [], []
                for oo in (o, o + 1):
                    def spread(q, n):
                        return jnp.broadcast_to(PRE[oo, q, pl.ds(i, 1), :], (n, LANES))

                    here = a_iota == spread(9, 8)
                    cols = []
                    for q in range(2 * FOOT):
                        cols.append(jnp.where(here, spread(q, 8), 0.0))
                    lhs.append(jnp.concatenate(cols, 0).astype(BF16))
                    hot = n_iota == jnp.broadcast_to(spread(8, 16).astype(BF16)[:1], (LANES, LANES))
                    rhs.append(jnp.where(hot, jnp.ones((), BF16), jnp.zeros((), BF16)))
                acc = acc + lax.dot_general(
                    jnp.concatenate(lhs, 1),
                    jnp.concatenate(rhs, 1),
                    (((1,), (1,)), ((), ())),
                    preferred_element_type=F32,
                )
            sums = [acc[16 * j:16 * j + 8] + acc[16 * j + 8:16 * j + 16] for j in range(FOOT)]

            @pl.when(k < NI)
            def _():
                for j in range(FOOT):
                    sendB[t, k - 1, j] = sums[j]
                pltpu.make_async_remote_copy(
                    src_ref=sendB.at[t, k - 1],
                    dst_ref=recvB.at[t, k - 1],
                    send_sem=b_send,
                    recv_sem=b_recv.at[t],
                    device_id=(y * NI + i, z),
                    device_id_type=MESH,
                ).start()

            @pl.when(k == NI)
            def _():
                for j in range(FOOT):
                    recvB[t, NI - 1, j] = sums[j]

            return carry

        lax.fori_loop(1, NI + 1, tile, 0)

    def forcing(t):
        pltpu.make_async_copy(
            recvB.at[t, pl.ds(0, NI - 1)], recvB.at[t, pl.ds(0, NI - 1)], b_recv.at[t]
        ).wait()
        xs = []
        for j in range(FOOT):
            x = recvB[t, 0, j]
            for k in range(1, NI):
                x = x + recvB[t, k, j]
            xs.append(x)
        x = jnp.concatenate(xs, 1)
        hi = x.astype(BF16).astype(F32)
        both = jnp.concatenate([hi, x - hi], 0).astype(BF16)
        f = jnp.dot(both, E[...], preferred_element_type=F32)
        f = f[:8] + f[8:]
        return [
            jnp.concatenate(
                [f[:, h * LANES:(h + 1) * LANES], f[:, 256 + h * LANES:256 + (h + 1) * LANES]], 0
            )
            for h in range(HALVES)
        ]

    def edge_copies(t):
        return [
            pltpu.make_async_remote_copy(
                src_ref=HS.at[t, pl.ds(first, many)],
                dst_ref=HR.at[t, pl.ds(first, many)],
                send_sem=h_send,
                recv_sem=h_recv.at[t],
                device_id=to,
                device_id_type=MESH,
            )
            for first, many, to in routes
        ]

    V2 = V.reshape(HALVES * NZ * ROWS * 2, LANES)

    def send_edges(t, p4, p5):
        slot = t % 2
        for h in range(HALVES):
            base = (slot * HALVES + h) * NZ * ROWS
            HS[t, h] = V2[pl.ds(base + ROWS - 1, NZ, stride=ROWS), :]
            HS[t, 2 + h] = V2[pl.ds(base, NZ, stride=ROWS), :]
        HS[t, 4] = p4
        HS[t, 5] = p5
        for c in edge_copies(t):
            c.start()

    def stencil(t, put):
        slot = t % 2
        pltpu.make_async_copy(HR.at[t], HR.at[t], h_recv.at[t]).wait()
        lefts = HR[t, 4]
        rights = HR[t, 5]
        for l in range(NZ):
            halves = [V[slot, 0, l], V[slot, 1, l]]
            made = []
            for h in range(HALVES):
                near = around(
                    halves,
                    [HR[t, g, pl.ds(l, 1), :] for g in (0, 1)],
                    [HR[t, g, pl.ds(l, 1), :] for g in (2, 3)],
                    lefts[:, l:l + 1],
                    rights[:, l:l + 1],
                    h,
                )
                terms = [CF[t, 0, h, l] * halves[h]]
                terms += [CF[t, 1 + n, h, l] * near[n] for n in range(4)]
                if l > 0:
                    terms.append(CF[t, 5, h, l] * V[slot, h, l - 1])
                if l < NZ - 1:
                    terms.append(CF[t, 6, h, l] * V[slot, h, l + 1])
                total = terms[0]
                for term in terms[1:]:
                    total = total + term
                made.append(total)
            put(l, made)

    def first_edges():
        t = STEPS - 1
        f = forcing(t)
        p4 = jnp.where(lane == 0, f[1][:, LANES - 1:], 0.0)
        p5 = jnp.where(lane == 0, f[0][:, :1], 0.0)
        for h in range(HALVES):
            V[t % 2, h, 0] = f[h]
        send_edges(t, p4, p5)

    gather(STEPS - 1)
    gather(STEPS - 2)
    first_edges()

    def advance(s, carry):
        t = STEPS - 1 - s

        @pl.when(t >= 2)
        def _():
            gather(t - 2)

        f = forcing(t - 1)
        ps = [jnp.zeros((ROWS, LANES), F32), jnp.zeros((ROWS, LANES), F32)]

        def put(l, made):
            if l == 0:
                made = [made[h] + f[h] for h in range(HALVES)]
            for h in range(HALVES):
                V[(t - 1) % 2, h, l] = made[h]
            ps[0] = jnp.where(lane == l, made[1][:, LANES - 1:], ps[0])
            ps[1] = jnp.where(lane == l, made[0][:, :1], ps[1])

        stencil(t, put)
        send_edges(t - 1, ps[0], ps[1])
        return carry

    lax.fori_loop(0, STEPS - 1, advance, 0)

    def last(l, made):
        for h in range(HALVES):
            out[l, :, h * LANES:(h + 1) * LANES] = made[h] + BG[h, l]

    stencil(0, last)

    for c in state_copies():
        c.wait_send()

    def drained(buf, sem):
        pltpu.make_async_remote_copy(
            src_ref=buf, dst_ref=buf, send_sem=sem, recv_sem=sem,
            device_id=(down, z), device_id_type=MESH,
        ).wait_send()

    drained(sendA, a_send)
    drained(sendB, b_send)
    drained(HS, h_send)


def shards(sv, bg, res, wgt, ker, cell, cnt):
    def by_step(x):
        return jnp.transpose(x[0], (1, 0, 2)).reshape(STEPS * LANES, LANES)

    anyspace = pl.BlockSpec(memory_space=pl.ANY)
    vmem = pl.BlockSpec(memory_space=pltpu.VMEM)
    dma = pltpu.SemaphoreType.DMA
    return pl.pallas_call(
        kernel,
        out_shape=jax.ShapeDtypeStruct(bg.shape, F32),
        in_specs=[anyspace] * 6 + [vmem],
        out_specs=vmem,
        scratch_shapes=[
            pltpu.VMEM((STEPS + 1, HALVES, NZ, ROWS, LANES), F32),
            pltpu.VMEM((STEPS * LANES, LANES), F32),
            pltpu.VMEM((STEPS * LANES, LANES), F32),
            pltpu.VMEM((STEPS * LANES, LANES), jnp.int32),
            pltpu.VMEM((STEPS * LANES * FOOT, LANES), F32),
            pltpu.VMEM((LANES, LANES), F32),
            pltpu.VMEM((STEPS, NA - 1, FOOT + 1, NI, LANES), F32),
            pltpu.VMEM((STEPS, NA, FOOT + 1, NI, LANES), F32),
            pltpu.VMEM((STEPS, NI - 1, FOOT, 8, LANES), F32),
            pltpu.VMEM((STEPS, NI, FOOT, 8, LANES), F32),
            pltpu.VMEM((STEPS + 1, 6, NZ, LANES), F32),
            pltpu.VMEM((STEPS + 1, 6, NZ, LANES), F32),
            pltpu.VMEM((STEPS, 6, NZ, LANES), F32),
            pltpu.VMEM((STEPS, 6, NZ, LANES), F32),
            pltpu.VMEM((STEPS, 7, HALVES, NZ, ROWS, LANES), F32),
            pltpu.VMEM((HALVES, NZ, ROWS, LANES), F32),
            pltpu.VMEM((HALVES, NZ, ROWS, LANES), F32),
            pltpu.VMEM((2, HALVES, NZ, ROWS, LANES), F32),
            pltpu.VMEM((512, 512), BF16),
            pltpu.VMEM((NA, 2 * FOOT + 2, NI, LANES), F32),
            dma((4,)), dma((4,)), dma, dma((STEPS,)), dma, dma((STEPS,)),
            dma((4,)), dma((4,)), dma, dma((STEPS,)),
        ],
        compiler_params=pltpu.CompilerParams(
            collective_id=0, has_side_effects=True, vmem_limit_bytes=48 * 1024 * 1024
        ),
        cost_estimate=pl.CostEstimate(
            flops=2_000_000_000, bytes_accessed=8_000_000, transcendentals=0
        ),
    )(
        sv, bg, by_step(res), by_step(wgt), by_step(cell),
        ker.reshape(STEPS * LANES * FOOT, LANES), jnp.transpose(cnt[0], (1, 0)),
    )


def solution(mesh):
    in_specs = (
        P(None, None, "lat", "swath"),
        P(None, "lat", "swath"),
        P(("lat", "swath"), None, None, None),
        P(("lat", "swath"), None, None, None),
        P(("lat", "swath"), None, None, None, None),
        P(("lat", "swath"), None, None, None),
        P(("lat", "swath"), None, None),
    )
    return jax.shard_map(
        shards, mesh=mesh, in_specs=in_specs, out_specs=P(None, "lat", "swath"), check_vma=False
    )
```

profile of v0, /device:TPU:0, one launch (start us, length us, event | category | flops | bytes accessed | tf_op | source)
XLA Modules:
  0.0 62.9 jit_solution(2483610711716446046)
XLA Ops:
  0.0 0.7 %copy.10 = s32[1,128,6]{1,2,0:T(8,128)S(1)} copy(s32[1,128,6]{1,0,2:T(1,128)} %param.13) | data formatting | bytes 6144
  0.7 0.0 copy-start
  0.7 1.4 %copy-done = f32[6,16,16,256]{3,2,1,0:T(8,128)S(1)} copy-done((f32[6,16,16,256]{3,2,1,0:T(8,128)S(1)}, f32[6,16,16,256]{3,2,1,0:T(8,128)}, u32[]{:S(2)}) %copy-start) | copy-done | bytes 1572888
  2.1 0.0 copy-start.1
  2.1 1.4 %copy-done.1 = f32[1,128,6,4,128]{4,3,2,1,0:T(4,128)S(1)} copy-done((f32[1,128,6,4,128]{4,3,2,1,0:T(4,128)S(1)}, f32[1,128,6,4,128]{4,3,2,1,0:T(4,128)}, u32[]{:S(2)}) %copy-start.1) | copy-done | bytes 1572888
  3.5 0.0 copy-start.2
  3.5 1.0 %copy-done.2 = f32[1,128,6,128]{3,1,2,0:T(8,128)S(1)} copy-done((f32[1,128,6,128]{3,1,2,0:T(8,128)S(1)}, f32[1,128,6,128]{3,1,2,0:T(8,128)}, u32[]{:S(2)}) %copy-start.2) | copy-done | bytes 393240
  4.5 0.0 copy-start.3
  4.5 1.0 %copy-done.3 = f32[1,128,6,128]{3,1,2,0:T(8,128)S(1)} copy-done((f32[1,128,6,128]{3,1,2,0:T(8,128)S(1)}, f32[1,128,6,128]{3,1,2,0:T(8,128)}, u32[]{:S(2)}) %copy-start.3) | copy-done | bytes 393240
  5.5 0.0 copy-start.4
  5.5 1.0 %copy-done.4 = s32[1,128,6,128]{3,1,2,0:T(8,128)S(1)} copy-done((s32[1,128,6,128]{3,1,2,0:T(8,128)S(1)}, s32[1,128,6,128]{3,1,2,0:T(8,128)}, u32[]{:S(2)}) %copy-start.4) | copy-done | bytes 393240
  6.5 0.0 copy-start.5
  6.5 0.9 %copy-done.5 = f32[16,16,256]{2,1,0:T(8,128)S(1)} copy-done((f32[16,16,256]{2,1,0:T(8,128)S(1)}, f32[16,16,256]{2,1,0:T(8,128)}, u32[]{:S(2)}) %copy-start.5) | copy-done | bytes 262168
  7.4 54.8 %shard_map.73 = f32[16,16,256]{2,1,0:T(8,128)S(1)} custom-call(f32[6,16,16,256]{3,2,1,0:T(8,128)S(1)} %copy-done, f32[16,16,256]{2,1,0:T(8,128)S(1)} %copy-done.5, f32[768,128]{1,0:T(8,128)S(1)} %bitcast.23, f32[768,128]{1,0:T(8,128)S(1)} %bitcast.24, s32[768,128]{1,0:T(8,128)S(1)} %bitcast.25, f32[3072,128]{1,0:T(8,128)S(1)} %bitcast.22, s32[6,128]{1,0:T(8,128)S(1)} %bitcast.21), custom_call_target="tpu_custom_call" | custom-call | flops 2000000000 | bytes 8000000 | tf_op jit(solution)/shard_map/pallas_call | solution.py:474
  62.2 0.7 %copy.12 = f32[16,16,256]{2,1,0:T(8,128)} copy(f32[16,16,256]{2,1,0:T(8,128)S(1)} %shard_map.73) | data formatting | bytes 524288
Async XLA Ops:
  0.7 1.4 %copy-start = (f32[6,16,16,256]{3,2,1,0:T(8,128)S(1)}, f32[6,16,16,256]{3,2,1,0:T(8,128)}, u32[]{:S(2)}) copy-start(f32[6,16,16,256]{3,2,1,0:T(8,128)} %sv.1) | copy-start | bytes 4718596
  2.1 1.4 %copy-start.1 = (f32[1,128,6,4,128]{4,3,2,1,0:T(4,128)S(1)}, f32[1,128,6,4,128]{4,3,2,1,0:T(4,128)}, u32[]{:S(2)}) copy-start(f32[1,128,6,4,128]{4,3,2,1,0:T(4,128)} %param.11) | copy-start | bytes 4718596
  3.5 1.0 %copy-start.2 = (f32[1,128,6,128]{3,1,2,0:T(8,128)S(1)}, f32[1,128,6,128]{3,1,2,0:T(8,128)}, u32[]{:S(2)}) copy-start(f32[1,128,6,128]{3,1,2,0:T(8,128)} %param.9) | copy-start | bytes 1179652
  4.5 1.0 %copy-start.3 = (f32[1,128,6,128]{3,1,2,0:T(8,128)S(1)}, f32[1,128,6,128]{3,1,2,0:T(8,128)}, u32[]{:S(2)}) copy-start(f32[1,128,6,128]{3,1,2,0:T(8,128)} %param.10) | copy-start | bytes 1179652
  5.5 1.0 %copy-start.4 = (s32[1,128,6,128]{3,1,2,0:T(8,128)S(1)}, s32[1,128,6,128]{3,1,2,0:T(8,128)}, u32[]{:S(2)}) copy-start(s32[1,128,6,128]{3,1,2,0:T(8,128)} %param.12) | copy-start | bytes 1179652
  6.5 0.9 %copy-start.5 = (f32[16,16,256]{2,1,0:T(8,128)S(1)}, f32[16,16,256]{2,1,0:T(8,128)}, u32[]{:S(2)}) copy-start(f32[16,16,256]{2,1,0:T(8,128)} %bg.1) | copy-start | bytes 786436
where the time goes:
time: 63.3 us; the launch traced here: 62.9 us
  Pallas kernels  54.8 us (87%)
  local copies, waits for them, and re-layouts  8.14 us (13%)
    pallas_call x1, Pallas kernels, shards(): pl.pallas_call(kernel, out_shape=jax.ShapeDtypeStruct(bg.shape, F32), in_...  54.8 us
    unnamed x14, local copies, waits for them, and re-layouts  8.14 us

commit v1 on v0

v1 whole, which is shorter than its diff:
```python
import functools

import jax
import jax.numpy as jnp
from jax import lax
from jax.experimental import pallas as pl
from jax.experimental.pallas import tpu as pltpu
from jax.sharding import PartitionSpec as P

MESH = pl.DeviceIdType.MESH
F32 = jnp.float32
BF16 = jnp.bfloat16

SAT = 0.45
STEPS = 6
NZ = 16
ROWS = 16
LANES = 128
HALVES = 2
FOOT = 4
WIDE = 3
TALL = 32

NY4 = 4
NI = 8
NZ4 = 4
NA = NY4 * NZ4


def iota(shape, dim):
    return lax.broadcasted_iota(jnp.int32, shape, dim)


def kernel(
    sv, bg, res, wgt, cell, ker, cnt, out,
    X, R, W, C, KV, CT, sendA, recvA, sendB, recvB, RS, RR, CS, CR, FS, FR,
    CF, KK, BG, V, E, PRE,
    in_sem, st_sem, a_send, a_recv, b_send, b_recv, s_send, s_recv, f_send, f_recv,
):
    lat = lax.axis_index("lat")
    z = lax.axis_index("swath")
    y = lat // NI
    me_i = lat % NI
    nlat = NY4 * NI

    loads = [
        pltpu.make_async_copy(res, R, in_sem.at[0]),
        pltpu.make_async_copy(wgt, W, in_sem.at[1]),
        pltpu.make_async_copy(cell, C, in_sem.at[2]),
        pltpu.make_async_copy(ker, KV, in_sem.at[3]),
    ]
    own = pl.ds(0, ROWS)
    states = []
    for h in range(HALVES):
        cols = pl.ds(h * LANES, LANES)
        states.append(
            pltpu.make_async_copy(
                sv.at[:, :, :, cols], X.at[pl.ds(0, STEPS), h, :, own], st_sem.at[h]
            )
        )
        states.append(
            pltpu.make_async_copy(bg.at[:, :, cols], X.at[STEPS, h, :, own], st_sem.at[2 + h])
        )
    for c in loads:
        c.start()
    for c in states:
        c.start()

    up = (lat + nlat - 1) % nlat
    down = (lat + 1) % nlat
    left = (z + NZ4 - 1) % NZ4
    right = (z + 1) % NZ4
    partners = []
    for r in range(1, NA):
        partners.append((((y + r // NZ4) % NY4) * NI + me_i, (z + r % NZ4) % NZ4))
    for k in range(1, NI):
        partners.append((y * NI + (me_i + k) % NI, z))
    for a in (up, down):
        for b in (left, z, right):
            partners.append((a, b))
    barrier = pltpu.get_barrier_semaphore()
    for to in partners:
        pl.semaphore_signal(barrier, inc=1, device_id=to, device_id_type=MESH)

    lane = iota((ROWS, LANES), 1)
    lane8 = iota((8, LANES), 1)
    laneT = iota((TALL, LANES), 1)
    rowT = iota((TALL, LANES), 0)

    counts = [cnt[t].astype(F32) for t in range(STEPS)]
    counts = jnp.concatenate(counts + [jnp.zeros((LANES - STEPS, LANES), F32)], 0)
    CT[...] = jnp.transpose(counts, (1, 0))

    def build(q, carry):
        rr = iota((LANES, 512), 0)
        cc = iota((LANES, 512), 1)
        hit = ((rr >> 6) == (cc >> 8)) & (((rr & 63) * FOOT + q) == (cc & 255))
        E[pl.ds(pl.multiple_of(q * LANES, LANES), LANES), :] = jnp.where(hit, 1.0, 0.0).astype(BF16)
        return carry

    lax.fori_loop(0, FOOT, build, 0)

    for c in loads:
        c.wait()

    lanef = iota((LANES, LANES), 1).astype(F32)
    for t in range(STEPS - 1, -1, -1):
        rows = pl.ds(t * LANES, LANES)
        R[rows, :] = jnp.where(lanef < CT[:, t:t + 1], R[rows, :] * W[rows, :], 0.0)

    def weigh(t, yp, zp):
        d0 = yp * 32 + zp
        rows = pl.ds(t * LANES + d0, NI, stride=4)
        scaled = R[rows, :]
        parts = [
            scaled * KV[pl.ds(d0 * STEPS * FOOT + t * FOOT + j, NI, stride=4 * STEPS * FOOT), :]
            for j in range(FOOT)
        ]
        return parts + [C[rows, :].astype(F32)]

    def partner(r):
        return (y + r // NZ4) % NY4, (z + r % NZ4) % NZ4

    def fill(t):
        for r in range(1, NA):
            for q, part in enumerate(weigh(t, *partner(r))):
                sendA[t, r - 1, q] = part
        for q, part in enumerate(weigh(t, y, z)):
            recvA[t, NA - 1, q] = part

    def stage_a_send(t):
        for r in range(1, NA):
            ty, tz = partner(r)
            pltpu.make_async_remote_copy(
                src_ref=sendA.at[t, r - 1],
                dst_ref=recvA.at[t, r - 1],
                send_sem=a_send,
                recv_sem=a_recv.at[t],
                device_id=(ty * NI + me_i, tz),
                device_id_type=MESH,
            ).start()

    fill(STEPS - 1)
    pl.semaphore_wait(barrier, len(partners))
    stage_a_send(STEPS - 1)

    for c in states:
        c.wait()

    X2 = X.reshape((STEPS + 1) * WIDE * NZ * TALL, LANES)
    widths = [t + 1 for t in range(STEPS)] + [1]
    slices = [(t, k) for t, w in enumerate(widths) for k in range(w)]
    for n, (t, k) in enumerate(slices):
        for h in range(HALVES):
            base = (t * WIDE + h) * NZ * TALL
            RS[0, n, h] = X2[pl.ds(base + ROWS - widths[t] + k, NZ, stride=TALL), :]
            RS[1, n, h] = X2[pl.ds(base + k, NZ, stride=TALL), :]

    def state_columns(t, carry):
        p = [jnp.zeros((ROWS, LANES), F32), jnp.zeros((ROWS, LANES), F32)]
        for l in range(NZ):
            here = (lane >= 8 * l) & (lane < 8 * l + 8)
            for h in range(HALVES):
                x = X[t, h, l, 0:ROWS, :]
                turn = (8 * l + (8 if h == 1 else 0)) % LANES
                if turn:
                    x = pltpu.roll(x, turn, 1)
                p[h] = jnp.where(here, x, p[h])
        for h in range(HALVES):
            for q in range(2):
                CS[h, q, t] = p[h][8 * q:8 * q + 8]
        return carry

    lax.fori_loop(0, STEPS + 1, state_columns, 0)

    def tile_routes(src, dst):
        every = slice(None)
        return [
            (src(every, 1), dst(0, 2), (down, z)),
            (src(every, 0), dst(2, 2), (up, z)),
            (src(1, every), dst(4, 2), (lat, right)),
            (src(0, every), dst(6, 2), (lat, left)),
            (src(1, 1), dst(8, 1), (down, right)),
            (src(0, 1), dst(9, 1), (down, left)),
            (src(1, 0), dst(10, 1), (up, right)),
            (src(0, 0), dst(11, 1), (up, left)),
        ]

    def state_copies():
        pairs = [(RS.at[0], RR.at[0], (down, z)), (RS.at[1], RR.at[1], (up, z))]
        pairs += tile_routes(
            lambda h, q: CS.at[h] if q == slice(None) else CS.at[h, q],
            lambda n, many: CR.at[pl.ds(n - 4, many)] if many == 2 else CR.at[n - 4],
        )[2:]
        return [
            pltpu.make_async_remote_copy(
                src_ref=src, dst_ref=dst, send_sem=s_send.at[n], recv_sem=s_recv.at[n],
                device_id=to, device_id_type=MESH,
            )
            for n, (src, dst, to) in enumerate(pairs)
        ]

    for c in state_copies():
        c.start()

    def stage_a_step(s, carry):
        t = STEPS - 1 - s
        fill(t)
        stage_a_send(t)
        return carry

    lax.fori_loop(1, STEPS, stage_a_step, 0)

    has_up = (lat > 0).astype(F32)
    has_down = (lat < nlat - 1).astype(F32)
    has_left = (z > 0).astype(F32)
    has_right = (z < NZ4 - 1).astype(F32)
    inside = jnp.where(rowT < ROWS, 1.0, jnp.where(rowT < ROWS + 8, has_down, has_up))
    sides = jnp.where(laneT < 64, has_right, has_left)
    masks = [inside, inside, inside * sides]

    def clear(t, carry):
        for g in range(HALVES):
            for l in range(NZ):
                X[t, g, l, ROWS:TALL, :] = jnp.zeros((TALL - ROWS, LANES), F32)
        return carry

    lax.fori_loop(0, STEPS + 1, clear, 0)

    for c in state_copies():
        c.wait_recv()

    for n, (t, k) in enumerate(slices):
        for h in range(HALVES):
            base = (t * WIDE + h) * NZ * TALL
            X2[pl.ds(base + TALL - widths[t] + k, NZ, stride=TALL), :] = RR[0, n, h] * has_up
            X2[pl.ds(base + ROWS + k, NZ, stride=TALL), :] = RR[1, n, h] * has_down

    def third(t, carry):
        from_left = jnp.concatenate([CR[0, t], CR[1, t], CR[6, t], CR[4, t]], 0)
        from_right = jnp.concatenate([CR[2, t], CR[3, t], CR[7, t], CR[5, t]], 0)
        from_left = from_left * (inside * has_left)
        from_right = from_right * (inside * has_right)
        for l in range(NZ):
            a = pltpu.roll(from_left, (120 - 8 * l) % LANES, 1) if l != 15 else from_left
            b = pltpu.roll(from_right, (LANES - 8 * l) % LANES, 1) if l else from_right
            X[t, 2, l] = jnp.where(laneT >= 120, a, jnp.where(laneT < 8, b, 0.0))
        return carry

    lax.fori_loop(0, STEPS + 1, third, 0)

    def to_right(xs):
        turned = [pltpu.roll(x, LANES - 1, 1) for x in xs]
        return [jnp.where(laneT == LANES - 1, turned[(g + 1) % WIDE], turned[g]) for g in range(WIDE)]

    def to_left(xs):
        turned = [pltpu.roll(x, 1, 1) for x in xs]
        return [jnp.where(laneT == 0, turned[(g + WIDE - 1) % WIDE], turned[g]) for g in range(WIDE)]

    def coefficients(s, carry):
        t = STEPS - 1 - s
        before = None
        for l in range(NZ):
            ks = []
            for g in range(WIDE):
                rel = X[t, g, l] * (1.0 / SAT)
                square = rel * rel
                CF[t, 3, g, l] = (0.03 * 3.0) * square
                ks.append(square * rel)
            beside = to_right(ks)
            for g in range(WIDE):
                CF[t, 0, g, l] = 0.05 * (ks[g] + beside[g])
                CF[t, 1, g, l] = 0.05 * (ks[g] + pltpu.roll(ks[g], TALL - 1, 0))
                if l > 0:
                    CF[t, 2, g, l - 1] = 0.125 * (before[g] + ks[g])
            before = ks
        return carry

    lax.fori_loop(0, STEPS, coefficients, 0)

    for l in range(NZ):
        xs = [X[STEPS, g, l] for g in range(WIDE)]
        rights = to_right(xs)
        lefts = to_left(xs)
        for h in range(HALVES):
            near = rights[h] + lefts[h] + (pltpu.roll(xs[h], TALL - 1, 0) + pltpu.roll(xs[h], 1, 0))
            BG[h, l] = (0.9 * xs[h] - 0.1 * near)[:ROWS]

    def blank(l, carry):
        for g in range(WIDE):
            V[(STEPS - 1) % 2, g, l] = jnp.zeros((TALL, LANES), F32)
        return carry

    lax.fori_loop(0, NZ, blank, 0)

    n_iota = iota((LANES, LANES), 0).astype(F32).astype(BF16)
    a_iota = iota((8, LANES), 0).astype(F32)

    def gather(t):
        pltpu.make_async_copy(
            recvA.at[t, pl.ds(0, NA - 1)], recvA.at[t, pl.ds(0, NA - 1)], a_recv.at[t]
        ).wait()

        def split(o, carry):
            anchor = recvA[t, o, FOOT]
            r = jnp.floor(anchor * (1.0 / 64.0))
            b = jnp.floor(anchor * (1.0 / 512.0))
            PRE[o, 8] = (anchor - 64.0 * r) + 64.0 * b
            PRE[o, 9] = r - 8.0 * b
            for j in range(FOOT):
                v = recvA[t, o, j]
                hi = v.astype(BF16).astype(F32)
                PRE[o, 2 * j] = hi
                PRE[o, 2 * j + 1] = v - hi
            return carry

        lax.fori_loop(0, NA, split, 0, unroll=True)

        def tile(k, carry):
            i = (me_i + k) % NI
            def spread(o, q, n):
                return jnp.broadcast_to(PRE[o, q, pl.ds(i, 1), :], (n, LANES))

            lhs, rhs = [], []
            for o in range(NA):
                here = a_iota == spread(o, 9, 8)
                cols = [jnp.where(here, spread(o, q, 8), 0.0) for q in range(2 * FOOT)]
                lhs.append(jnp.concatenate(cols, 0).astype(BF16))
                n_of = jnp.broadcast_to(spread(o, 8, 16).astype(BF16)[:1], (LANES, LANES))
                rhs.append(jnp.where(n_iota == n_of, jnp.ones((), BF16), jnp.zeros((), BF16)))
            acc = lax.dot_general(
                jnp.concatenate(lhs, 1),
                jnp.concatenate(rhs, 1),
                (((1,), (1,)), ((), ())),
                preferred_element_type=F32,
            )
            sums = [acc[16 * j:16 * j + 8] + acc[16 * j + 8:16 * j + 16] for j in range(FOOT)]

            @pl.when(k < NI)
            def _():
                for j in range(FOOT):
                    sendB[t, k - 1, j] = sums[j]
                pltpu.make_async_remote_copy(
                    src_ref=sendB.at[t, k - 1],
                    dst_ref=recvB.at[t, k - 1],
                    send_sem=b_send,
                    recv_sem=b_recv.at[t],
                    device_id=(y * NI + i, z),
                    device_id_type=MESH,
                ).start()

            @pl.when(k == NI)
            def _():
                for j in range(FOOT):
                    recvB[t, NI - 1, j] = sums[j]

            return carry

        lax.fori_loop(1, NI + 1, tile, 0)

    def surface_copies(t):
        def dst(n, many):
            return FR.at[t, pl.ds(n, many)] if many == 2 else FR.at[t, n]

        return [
            pltpu.make_async_remote_copy(
                src_ref=src, dst_ref=to_ref, send_sem=f_send, recv_sem=f_recv.at[t],
                device_id=to, device_id_type=MESH,
            )
            for src, to_ref, to in tile_routes(lambda h, q: FS.at[t, h, q], dst)
        ]

    def forcing(t):
        pltpu.make_async_copy(
            recvB.at[t, pl.ds(0, NI - 1)], recvB.at[t, pl.ds(0, NI - 1)], b_recv.at[t]
        ).wait()
        xs = []
        for j in range(FOOT):
            x = recvB[t, 0, j]
            for k in range(1, NI):
                x = x + recvB[t, k, j]
            xs.append(x)
        x = jnp.concatenate(xs, 1)
        hi = x.astype(BF16).astype(F32)
        both = jnp.concatenate([hi, x - hi], 0).astype(BF16)
        f = jnp.dot(both, E[...], preferred_element_type=F32)
        f = f[:8] + f[8:]
        for h in range(HALVES):
            for q in range(2):
                FS[t, h, q] = f[:, q * 256 + h * LANES:q * 256 + (h + 1) * LANES]
        for c in surface_copies(t):
            c.start()

    def add_surface(t):
        pltpu.make_async_copy(FR.at[t], FR.at[t], f_recv.at[t]).wait()
        wide = [
            jnp.concatenate([FS[t, h, 0], FS[t, h, 1], FR[t, 2 + h], FR[t, h]], 0)
            for h in range(HALVES)
        ]
        sided = [
            jnp.where(lane8 < 64, FR[t, b], FR[t, a])
            for a, b in ((4, 6), (5, 7), (10, 11), (8, 9))
        ]
        wide.append(jnp.concatenate(sided, 0))
        for g in range(WIDE):
            V[t % 2, g, 0] = V[t % 2, g, 0] + wide[g] * masks[g]

    def stencil(t, put):
        slot = t % 2
        add_surface(t)
        over = None
        vs = [V[slot, g, 0] for g in range(WIDE)]
        for l in range(NZ):
            beneath = [V[slot, g, l + 1] for g in range(WIDE)] if l < NZ - 1 else None
            beside = to_right(vs)
            across = [CF[t, 0, g, l] * (beside[g] - vs[g]) for g in range(WIDE)]
            behind = to_left(across)
            made, under = [], []
            for g in range(WIDE):
                v = vs[g]
                along = CF[t, 1, g, l] * (pltpu.roll(v, TALL - 1, 0) - v)
                total = v + (across[g] - behind[g]) + (along - pltpu.roll(along, 1, 0))
                if l < NZ - 1:
                    drop = beneath[g] - v
                    flux = CF[t, 2, g, l] * drop
                    total = total + (flux + CF[t, 3, g, l] * drop)
                    under.append(flux)
                else:
                    total = total - CF[t, 3, g, l] * v
                if l > 0:
                    total = total - over[g]
                made.append(total)
            put(l, made)
            over = under
            vs = beneath

    def step_to_next(t):
        def put(l, made):
            for g in range(WIDE):
                V[(t - 1) % 2, g, l] = made[g] * masks[g]

        stencil(t, put)

    gather(STEPS - 1)
    gather(STEPS - 2)
    forcing(STEPS - 1)

    def advance(s, carry):
        t = STEPS - 1 - s
        gather(t - 2)
        forcing(t - 1)
        step_to_next(t)
        return carry

    lax.fori_loop(0, STEPS - 2, advance, 0)
    forcing(0)
    step_to_next(1)

    def last(l, made):
        for h in range(HALVES):
            out[l, :, h * LANES:(h + 1) * LANES] = made[h][:ROWS] + BG[h, l]

    stencil(0, last)

    for c in state_copies():
        c.wait_send()

    def drained(buf, sem):
        pltpu.make_async_remote_copy(
            src_ref=buf, dst_ref=buf, send_sem=sem, recv_sem=sem,
            device_id=(down, z), device_id_type=MESH,
        ).wait_send()

    drained(sendA, a_send)
    drained(sendB, b_send)
    for t in range(STEPS):
        for c in surface_copies(t):
            c.wait_send()


def shards(sv, bg, res, wgt, ker, cell, cnt):
    def by_step(x):
        return jnp.transpose(x[0], (1, 0, 2)).reshape(STEPS * LANES, LANES)

    anyspace = pl.BlockSpec(memory_space=pltpu.HBM)
    vmem = pl.BlockSpec(memory_space=pltpu.VMEM)
    dma = pltpu.SemaphoreType.DMA
    return pl.pallas_call(
        kernel,
        out_shape=jax.ShapeDtypeStruct(bg.shape, F32),
        in_specs=[anyspace] * 6 + [vmem],
        out_specs=vmem,
        scratch_shapes=[
            pltpu.VMEM((STEPS + 1, WIDE, NZ, TALL, LANES), F32),
            pltpu.VMEM((STEPS * LANES, LANES), F32),
            pltpu.VMEM((STEPS * LANES, LANES), F32),
            pltpu.VMEM((STEPS * LANES, LANES), jnp.int32),
            pltpu.VMEM((STEPS * LANES * FOOT, LANES), F32),
            pltpu.VMEM((LANES, LANES), F32),
            pltpu.VMEM((STEPS, NA - 1, FOOT + 1, NI, LANES), F32),
            pltpu.VMEM((STEPS, NA, FOOT + 1, NI, LANES), F32),
            pltpu.VMEM((STEPS, NI - 1, FOOT, 8, LANES), F32),
            pltpu.VMEM((STEPS, NI, FOOT, 8, LANES), F32),
            pltpu.VMEM((2, 22, HALVES, NZ, LANES), F32),
            pltpu.VMEM((2, 22, HALVES, NZ, LANES), F32),
            pltpu.VMEM((HALVES, 2, STEPS + 1, 8, LANES), F32),
            pltpu.VMEM((8, STEPS + 1, 8, LANES), F32),
            pltpu.VMEM((STEPS, HALVES, 2, 8, LANES), F32),
            pltpu.VMEM((STEPS, 12, 8, LANES), F32),
            pltpu.VMEM((STEPS, 4, WIDE, NZ, TALL, LANES), F32),
            pltpu.VMEM((8, LANES), F32),
            pltpu.VMEM((HALVES, NZ, ROWS, LANES), F32),
            pltpu.VMEM((2, WIDE, NZ, TALL, LANES), F32),
            pltpu.VMEM((512, 512), BF16),
            pltpu.VMEM((NA, 2 * FOOT + 2, NI, LANES), F32),
            dma((4,)), dma((4,)), dma, dma((STEPS,)), dma, dma((STEPS,)),
            dma((8,)), dma((8,)), dma, dma((STEPS,)),
        ],
        compiler_params=pltpu.CompilerParams(
            collective_id=0, has_side_effects=True, vmem_limit_bytes=65200 * 1024
        ),
        cost_estimate=pl.CostEstimate(
            flops=2_000_000_000, bytes_accessed=8_000_000, transcendentals=0
        ),
    )(
        sv, bg, by_step(res), by_step(wgt), by_step(cell),
        ker.reshape(STEPS * LANES * FOOT, LANES), jnp.transpose(cnt, (2, 0, 1)),
    )


def solution(mesh):
    in_specs = (
        P(None, None, "lat", "swath"),
        P(None, "lat", "swath"),
        P(("lat", "swath"), None, None, None),
        P(("lat", "swath"), None, None, None),
        P(("lat", "swath"), None, None, None, None),
        P(("lat", "swath"), None, None, None),
        P(("lat", "swath"), None, None),
    )
    return jax.shard_map(
        shards, mesh=mesh, in_specs=in_specs, out_specs=P(None, "lat", "swath"), check_vma=False
    )
```

time: 63.3 us -> 63.3 us (level)
  Pallas kernels: 54.8 us -> 61.5 us
  local copies, waits for them, and re-layouts: 8.14 us -> 1.67 us
    pallas_call x1, Pallas kernels: 54.8 us -> 61.5 us  [shards(): pl.pallas_call(kernel, out_shape=jax.ShapeDtypeStruct(bg.shape, F32), in_...]
    unnamed x14 -> x1, local copies, waits for them, and re-layouts: 8.14 us -> 1.67 us
where the time goes in v1:
time: 63.3 us; the launch traced here: 63.2 us
  Pallas kernels  61.5 us (97%)
  local copies, waits for them, and re-layouts  1.67 us (3%)
    pallas_call x1, Pallas kernels, shards(): pl.pallas_call(kernel, out_shape=jax.ShapeDtypeStruct(bg.shape, F32), in_...  61.5 us
    unnamed x1, local copies, waits for them, and re-layouts  1.67 us

profile of v1, /device:TPU:0, one launch (start us, length us, event | category | flops | bytes accessed | tf_op | source)
XLA Modules:
  0.0 63.2 jit_solution(1994162217245796096)
XLA Ops:
  0.0 61.5 %shard_map.73 = f32[16,16,256]{2,1,0:T(8,128)} custom-call(f32[6,16,16,256]{3,2,1,0:T(8,128)} %sv.1, f32[16,16,256]{2,1,0:T(8,128)} %bg.1, f32[768,128]{1,0:T(8,128)} %bitcast.18, f32[768,128]{1,0:T(8,128)} %bitcast.19, s32[768,128]{1,0:T(8,128)} %bitcast.20, f32[3072,128]{1,0:T(8,128)} %bitcast.17, s32[6,1,128]{2,1,0:T(1,128)} %bitcast.21), custom_call_target="tpu_custom_call" | custom-call | flops 2000000000 | bytes 8000000 | tf_op jit(solution)/shard_map/pallas_call | solution.py:488
  61.5 1.7 %copy.9 = f32[16,16,256]{2,1,0:T(8,128)} copy(f32[16,16,256]{2,1,0:T(8,128)} %shard_map.73) | data formatting | bytes 524288

commit v2 on v1

--- a/solution.py
+++ b/solution.py
@@ -209,7 +209,9 @@
         stage_a_send(t)
         return carry
 
-    lax.fori_loop(1, STEPS, stage_a_step, 0)
+    lax.fori_loop(1, 2, stage_a_step, 0)
+    for t in range(STEPS - 2):
+        fill(t)
 
     has_up = (lat > 0).astype(F32)
     has_down = (lat < nlat - 1).astype(F32)
@@ -441,20 +443,27 @@
 
         stencil(t, put)
 
-    gather(STEPS - 1)
-    gather(STEPS - 2)
-    forcing(STEPS - 1)
-
-    def advance(s, carry):
-        t = STEPS - 1 - s
-        gather(t - 2)
-        forcing(t - 1)
-        step_to_next(t)
-        return carry
-
-    lax.fori_loop(0, STEPS - 2, advance, 0)
-    forcing(0)
-    step_to_next(1)
+    def slot(s, carry):
+
+        @pl.when(s < STEPS - 2)
+        def _():
+            stage_a_send(STEPS - 1 - 2 - s)
+
+        @pl.when(s < STEPS)
+        def _():
+            gather(STEPS - 1 - s)
+
+        @pl.when((s >= 2) & (s < STEPS + 2))
+        def _():
+            forcing(STEPS - 1 + 2 - s)
+
+        @pl.when(s >= 4)
+        def _():
+            step_to_next(STEPS - 1 + 4 - s)
+
+        return carry
+
+    lax.fori_loop(0, STEPS - 1 + 4, slot, 0)
 
     def last(l, made):
         for h in range(HALVES):

time: 63.3 us -> 56.3 us (0.89)
  Pallas kernels: 61.5 us -> 54.5 us
    pallas_call x1, Pallas kernels: 61.5 us -> 54.5 us  [shards(): pl.pallas_call(kernel, out_shape=jax.ShapeDtypeStruct(bg.shape, F32), in_...]
where the time goes in v2:
time: 56.3 us; the launch traced here: 56.2 us
  Pallas kernels  54.5 us (97%)
  local copies, waits for them, and re-layouts  1.67 us (3%)
    pallas_call x1, Pallas kernels, shards(): pl.pallas_call(kernel, out_shape=jax.ShapeDtypeStruct(bg.shape, F32), in_...  54.5 us
    unnamed x1, local copies, waits for them, and re-layouts  1.67 us

profile of v2, /device:TPU:0, one launch (start us, length us, event | category | flops | bytes accessed | tf_op | source)
XLA Modules:
  0.0 56.2 jit_solution(9759216907897483967)
XLA Ops:
  0.0 54.5 %shard_map.73 = f32[16,16,256]{2,1,0:T(8,128)} custom-call(f32[6,16,16,256]{3,2,1,0:T(8,128)} %sv.1, f32[16,16,256]{2,1,0:T(8,128)} %bg.1, f32[768,128]{1,0:T(8,128)} %bitcast.18, f32[768,128]{1,0:T(8,128)} %bitcast.19, s32[768,128]{1,0:T(8,128)} %bitcast.20, f32[3072,128]{1,0:T(8,128)} %bitcast.17, s32[6,1,128]{2,1,0:T(1,128)} %bitcast.21), custom_call_target="tpu_custom_call" | custom-call | flops 2000000000 | bytes 8000000 | tf_op jit(solution)/shard_map/pallas_call | solution.py:497
  54.5 1.7 %copy.9 = f32[16,16,256]{2,1,0:T(8,128)} copy(f32[16,16,256]{2,1,0:T(8,128)} %shard_map.73) | data formatting | bytes 524288

commit v3 on v2

--- a/solution.py
+++ b/solution.py
@@ -141,8 +141,6 @@
             ).start()
 
     fill(STEPS - 1)
-    pl.semaphore_wait(barrier, len(partners))
-    stage_a_send(STEPS - 1)
 
     for c in states:
         c.wait()
@@ -200,8 +198,10 @@
             for n, (src, dst, to) in enumerate(pairs)
         ]
 
+    pl.semaphore_wait(barrier, len(partners))
     for c in state_copies():
         c.start()
+    stage_a_send(STEPS - 1)
 
     def stage_a_step(s, carry):
         t = STEPS - 1 - s
@@ -209,8 +209,8 @@
         stage_a_send(t)
         return carry
 
-    lax.fori_loop(1, 2, stage_a_step, 0)
-    for t in range(STEPS - 2):
+    lax.fori_loop(1, 3, stage_a_step, 0)
+    for t in range(STEPS - 3):
         fill(t)
 
     has_up = (lat > 0).astype(F32)
@@ -445,9 +445,9 @@
 
     def slot(s, carry):
 
-        @pl.when(s < STEPS - 2)
+        @pl.when(s < STEPS - 3)
         def _():
-            stage_a_send(STEPS - 1 - 2 - s)
+            stage_a_send(STEPS - 1 - 3 - s)
 
         @pl.when(s < STEPS)
         def _():
@@ -457,13 +457,13 @@
         def _():
             forcing(STEPS - 1 + 2 - s)
 
-        @pl.when(s >= 4)
+        @pl.when(s >= 5)
         def _():
-            step_to_next(STEPS - 1 + 4 - s)
-
-        return carry
-
-    lax.fori_loop(0, STEPS - 1 + 4, slot, 0)
+            step_to_next(STEPS - 1 + 5 - s)
+
+        return carry
+
+    lax.fori_loop(0, STEPS - 1 + 5, slot, 0)
 
     def last(l, made):
         for h in range(HALVES):

time: 56.3 us -> 53.6 us (0.952); the launches traced: 56.2 us -> 52.5 us
  Pallas kernels: 54.5 us -> 50.8 us
    pallas_call x1, Pallas kernels: 54.5 us -> 50.8 us  [shards(): pl.pallas_call(kernel, out_shape=jax.ShapeDtypeStruct(bg.shape, F32), in_...]
where the time goes in v3:
time: 53.6 us; the launch traced here: 52.5 us
  Pallas kernels  50.8 us (95%)
  local copies, waits for them, and re-layouts  1.67 us (3%)
    pallas_call x1, Pallas kernels, shards(): pl.pallas_call(kernel, out_shape=jax.ShapeDtypeStruct(bg.shape, F32), in_...  50.8 us
    unnamed x1, local copies, waits for them, and re-layouts  1.67 us

profile of v3, /device:TPU:0, one launch (start us, length us, event | category | flops | bytes accessed | tf_op | source)
XLA Modules:
  0.0 52.5 jit_solution(16039642785588238499)
XLA Ops:
  0.0 50.8 %shard_map.73 = f32[16,16,256]{2,1,0:T(8,128)} custom-call(f32[6,16,16,256]{3,2,1,0:T(8,128)} %sv.1, f32[16,16,256]{2,1,0:T(8,128)} %bg.1, f32[768,128]{1,0:T(8,128)} %bitcast.18, f32[768,128]{1,0:T(8,128)} %bitcast.19, s32[768,128]{1,0:T(8,128)} %bitcast.20, f32[3072,128]{1,0:T(8,128)} %bitcast.17, s32[6,1,128]{2,1,0:T(1,128)} %bitcast.21), custom_call_target="tpu_custom_call" | custom-call | flops 2000000000 | bytes 8000000 | tf_op jit(solution)/shard_map/pallas_call | solution.py:497
  50.9 1.7 %copy.9 = f32[16,16,256]{2,1,0:T(8,128)} copy(f32[16,16,256]{2,1,0:T(8,128)} %shard_map.73) | data formatting | bytes 524288

commit v4 on v3

--- a/solution.py
+++ b/solution.py
@@ -526,7 +526,7 @@
             dma((8,)), dma((8,)), dma, dma((STEPS,)),
         ],
         compiler_params=pltpu.CompilerParams(
-            collective_id=0, has_side_effects=True, vmem_limit_bytes=65200 * 1024
+            collective_id=0, has_side_effects=True, vmem_limit_bytes=54800 * 1024
         ),
         cost_estimate=pl.CostEstimate(
             flops=2_000_000_000, bytes_accessed=8_000_000, transcendentals=0

time: 53.6 us -> 51.9 us (0.968)
  Pallas kernels: 50.8 us -> 49.7 us
    pallas_call x1, Pallas kernels: 50.8 us -> 49.7 us  [shards(): pl.pallas_call(kernel, out_shape=jax.ShapeDtypeStruct(bg.shape, F32), in_...]
    unnamed x1 -> x3, local copies, waits for them, and re-layouts: 1.67 us -> 1.39 us
where the time goes in v4:
time: 51.9 us; the launch traced here: 51.1 us
  Pallas kernels  49.7 us (96%)
  local copies, waits for them, and re-layouts  1.39 us (3%)
    pallas_call x1, Pallas kernels, shards(): pl.pallas_call(kernel, out_shape=jax.ShapeDtypeStruct(bg.shape, F32), in_...  49.7 us
    unnamed x3, local copies, waits for them, and re-layouts  1.39 us

profile of v4, /device:TPU:0, one launch (start us, length us, event | category | flops | bytes accessed | tf_op | source)
XLA Modules:
  0.0 51.1 jit_solution(5431661316552938712)
XLA Ops:
  0.0 0.0 copy-start
  0.0 0.7 %copy-done = s32[1,128,6]{1,0,2:T(1,128)S(1)} copy-done((s32[1,128,6]{1,0,2:T(1,128)S(1)}, s32[1,128,6]{1,0,2:T(1,128)}, u32[]{:S(2)}) %copy-start) | copy-done | bytes 3096
  0.7 49.7 %shard_map.73 = f32[16,16,256]{2,1,0:T(8,128)S(1)} custom-call(f32[6,16,16,256]{3,2,1,0:T(8,128)} %sv.1, f32[16,16,256]{2,1,0:T(8,128)} %bg.1, f32[768,128]{1,0:T(8,128)} %bitcast.19, f32[768,128]{1,0:T(8,128)} %bitcast.20, s32[768,128]{1,0:T(8,128)} %bitcast.21, f32[3072,128]{1,0:T(8,128)} %bitcast.18, s32[6,1,128]{2,1,0:T(1,128)S(1)} %bitcast.17), custom_call_target="tpu_custom_call" | custom-call | flops 2000000000 | bytes 8000000 | tf_op jit(solution)/shard_map/pallas_call | solution.py:497
  50.4 0.7 %copy.9 = f32[16,16,256]{2,1,0:T(8,128)} copy(f32[16,16,256]{2,1,0:T(8,128)S(1)} %shard_map.73) | data formatting | bytes 524288
Async XLA Ops:
  0.0 0.7 %copy-start = (s32[1,128,6]{1,0,2:T(1,128)S(1)}, s32[1,128,6]{1,0,2:T(1,128)}, u32[]{:S(2)}) copy-start(s32[1,128,6]{1,0,2:T(1,128)} %param.13) | copy-start | bytes 9220
